TPU v7x, 512 devices: a whole 4x4x16 slice. The times are simulated.
512 devices in a mesh: line: 16 (over z), py: 8 (over y, core), pz: 4 (over x).
Axes of the slice: x: 4, y: 4, z: 16, core: 2. Of those that a mesh axis runs over, the one named last changes fastest.
Arguments:
- fluxes: float32 [3, 128, 5, 32, 512], P(None, 'line', None, 'py', 'pz'), may hold values from -6 to 6
- jacobian: float32 [128, 5, 5, 32, 512], P('line', None, None, 'py', 'pz'), may hold values from -48 to 48, as said below
- dissipation: float32 [128, 32, 512], P('line', 'py', 'pz'), may hold values from 0.1 to 2
Outputs:
- update: float32 [128, 5, 32, 512], P('line', None, 'py', 'pz')
Inputs may be any that keep to these rules, and one draw needn't show every extreme that they name: jacobian[i, a, b, j, k] equals jacobian[i, b, a, j, k].
All inputs are finite; a program needn't handle non-finite values.
Results may differ from a plain program's by a relative error of at most 0.0003.
Values sent between devices are 32-bit elements; how exact they have to be, the bound alone decides.
A program may use at most 64 MiB of HBM per device.

v0:
```python
import jax
import jax.numpy as jnp
from jax import lax
from jax.sharding import PartitionSpec as P


def padded_2(shard, sides, width):
    for axis, dim in sides:
        count, length = (lax.axis_size(axis), shard.shape[dim])
        up = [(i, (i + 1) % count) for i in range(count - 1)]
        down = [(j, i) for i, j in up]
        last = lax.slice_in_dim(shard, length - width, length, axis=dim)
        initial = lax.slice_in_dim(shard, 0, width, axis=dim)
        before = lax.ppermute(last, axis, up)
        after = lax.ppermute(initial, axis, down)
        shard = jnp.concatenate([before, shard, after], axis=dim)
    return shard


def from_behind(block, axis, distance):
    devices = range(lax.axis_size(axis))
    route = [(i - distance, i) for i in devices if i - distance in devices]
    return lax.ppermute(block, axis, route)


def mat_mul(left_mat, right_mat):
    extent = left_mat.shape[-2]
    total = left_mat[..., :, 0:1, :] * right_mat[..., 0:1, :, :]
    for index in range(1, extent):
        total = (
            total + left_mat[..., :, index : index + 1, :] * right_mat[..., index : index + 1, :, :]
        )
    return total


def mat_vec(left_mat, vector):
    extent = left_mat.shape[-2]
    total = left_mat[..., :, 0, :] * vector[..., 0:1, :]
    for index in range(1, extent):
        total = total + left_mat[..., :, index, :] * vector[..., index : index + 1, :]
    return total


def solve_small(matrix, sides):
    extent = matrix.shape[0]
    mat_rows = [matrix[index] for index in range(extent)]
    side_rows = [sides[index] for index in range(extent)]
    for column in range(extent):
        scaling = 1.0 / mat_rows[column][column]
        mat_rows[column] = mat_rows[column] * scaling[None]
        side_rows[column] = side_rows[column] * scaling[None]
        for target in range(extent):
            if target != column:
                factor = mat_rows[target][column]
                mat_rows[target] = mat_rows[target] - factor[None] * mat_rows[column]
                side_rows[target] = side_rows[target] - factor[None] * side_rows[column]
    return jnp.stack(side_rows)


def block_thomas(lower, diagonal, upper, right):

    def forward(carried, row):
        prev_upper, prev_right = carried
        lower_row, diag_row, upper_row, right_row = row
        pivot_mat = diag_row - mat_mul(lower_row, prev_upper)
        columns = upper_row.shape[1]
        joined = jnp.concatenate([upper_row, right_row - mat_mul(lower_row, prev_right)], axis=1)
        solved = solve_small(pivot_mat, joined)
        result = (solved[:, :columns], solved[:, columns:])
        return (result, result)

    start_state = (jnp.zeros_like(upper[0]), jnp.zeros_like(right[0]))
    _, (uppers, rights) = lax.scan(forward, start_state, (lower, diagonal, upper, right))

    def backward(later, row):
        upper_row, right_row = row
        result = right_row - mat_mul(upper_row, later)
        return (result, result)

    final_row = rights[-1]
    _, earlier = lax.scan(backward, final_row, (uppers[:-1], rights[:-1]), reverse=True)
    return jnp.concatenate([earlier, final_row[None]], axis=0)


def reduced_solve(all_lower, all_diag, all_right, all_upper, all_first):
    next_first = jnp.concatenate([all_first[1:], jnp.zeros_like(all_first[:1])], axis=0)
    reduced_diag = all_diag - mat_mul(all_upper, next_first[:, :, 1:6, :])
    reduced_upper = -mat_mul(all_upper, next_first[:, :, 6:11, :])
    reduced_right = all_right - mat_vec(all_upper, next_first[:, :, 0, :])
    return block_thomas(all_lower, reduced_diag, reduced_upper, reduced_right[:, :, None, :])[
        :, :, 0, :
    ]


def local_section(faces, diag_value, right, before, position, segments, identity):
    extent_x = faces.shape[0]
    lines = faces.shape[3]
    lower = -jnp.concatenate([before, faces[:-1]], axis=0)
    is_final = position == segments - 1
    upper = jnp.concatenate([faces[:-1], jnp.where(is_final, 0.0, faces[-1:])], axis=0)
    diagonal = identity[None, :, :, None] * diag_value[:, None, None, :]
    interior = extent_x - 1
    zero_block = jnp.zeros((interior, 5, 5, lines), jnp.float32)
    first_cols = zero_block.at[0].set(lower[0])
    last_cols = zero_block.at[interior - 1].set(upper[interior - 1])
    sides = jnp.concatenate([right[:interior, :, None, :], first_cols, last_cols], axis=2)
    local = block_thomas(lower[:interior], diagonal[:interior], upper[:interior], sides)
    sep_lower = lower[interior]
    own_lower = -mat_mul(sep_lower, local[-1, :, 1:6, :])
    own_diag = diagonal[interior] - mat_mul(sep_lower, local[-1, :, 6:11, :])
    own_right = right[interior] - mat_vec(sep_lower, local[-1, :, 0, :])
    return (local, own_lower, own_diag, own_right, upper[interior])


def finish_section(local, left_value, own_value):
    inner = local[:, :, 0, :] - mat_vec(local[:, :, 1:6, :], left_value[None])
    inner = inner - mat_vec(local[:, :, 6:11, :], own_value[None])
    return jnp.concatenate([inner, own_value[None]], axis=0)


def per_device(fluxes, jacobian, dissipation):
    extent_x = jacobian.shape[0]
    extent_y = jacobian.shape[3]
    extent_z = jacobian.shape[4]
    lines = extent_y * extent_z
    flux_x = padded_2(fluxes[0], (("line", 0),), 1)
    flux_y = padded_2(fluxes[1], (("py", 2),), 1)
    flux_z = padded_2(fluxes[2], (("pz", 3),), 1)
    right = -0.5 * (
        flux_x[2:]
        - flux_x[:-2]
        + (flux_y[:, :, 2:] - flux_y[:, :, :-2])
        + (flux_z[..., 2:] - flux_z[..., :-2])
    )
    right = right.reshape(extent_x, 5, lines)
    faces = jacobian.reshape(extent_x, 5, 5, lines)
    diag_value = 1.0 + dissipation.reshape(extent_x, lines)
    identity = jnp.eye(5, dtype=jnp.float32)
    position = lax.axis_index("line")
    segments = lax.axis_size("line")
    before = from_behind(faces[-1:], "line", 1)
    local, own_lower, own_diag, own_right, sep_upper = local_section(
        faces, diag_value, right, before, position, segments, identity
    )
    gathered = (
        lax.all_gather(own_lower[None], "line", axis=0, tiled=True),
        lax.all_gather(own_diag[None], "line", axis=0, tiled=True),
        lax.all_gather(own_right[None], "line", axis=0, tiled=True),
        lax.all_gather(sep_upper[None], "line", axis=0, tiled=True),
        lax.all_gather(local[:1], "line", axis=0, tiled=True),
    )
    all_lower, all_diag, all_right, all_upper, all_first = gathered
    separators = reduced_solve(all_lower, all_diag, all_right, all_upper, all_first)
    padded = jnp.concatenate([jnp.zeros_like(separators[:1]), separators], axis=0)
    left_value = lax.dynamic_index_in_dim(padded, position, 0, keepdims=False)
    own_value = lax.dynamic_index_in_dim(padded, position + 1, 0, keepdims=False)
    update = finish_section(local, left_value, own_value)
    return update.reshape(extent_x, 5, extent_y, extent_z)


def solution(mesh):
    return jax.shard_map(
        per_device,
        mesh=mesh,
        in_specs=(
            P(None, "line", None, "py", "pz"),
            P("line", None, None, "py", "pz"),
            P("line", "py", "pz"),
        ),
        out_specs=P("line", None, "py", "pz"),
        check_vma=False,
    )
```

profile of v0, /device:TPU:24, one launch (start us, length us, event | category | flops | bytes accessed | tf_op | source)
XLA Modules:
  0.0 309.4 jit_solution(9390370623037688757)
XLA Ops:
  6.5 1.1 slice_bitcast_fusion.42
  7.7 1.3 collective-permute-start.4
  9.0 4.6 %collective-permute-start.5 = (f32[8,5,4,1]{3,2,1,0:T(4,128)S(1)}, f32[8,5,4,1]{3,2,1,0:T(4,128)S(1)}, u32[]{:S(2)}, u32[]{:S(2)}) collective-permute-start(f32[8,5,4,1]{3,2,1,0:T(4,128)S(1)} %get-tuple-element.647), channel_id=1, source_target_pairs={{0,1},{1,2},{2,3},{4,5},{5,6},{6,7},{8,9},{9,10},{10,11},{12,13},{... | collective-permute-start | bytes 1928 | tf_op jit(solution)/shard_map/ppermute | solution.py:14
  13.6 1.9 collective-permute-start.2
  15.5 2.4 collective-permute-start.3
  18.7 1.3 collective-permute-start
  21.6 4.5 %collective-permute-start.1 = (f32[1,5,4,128]{3,2,1,0:T(4,128)S(1)}, f32[1,5,4,128]{3,2,1,0:T(4,128)S(1)}, u32[]{:S(2)}, u32[]{:S(2)}) collective-permute-start(f32[1,5,4,128]{3,2,1,0:T(4,128)S(1)} %get-tuple-element.616), channel_id=1, source_target_pairs={{0,32},{32,64},{64,96},{96,128},{128,160},{160,192},{192,224},{224... | collective-permute-start | bytes 30728 | tf_op jit(solution)/shard_map/ppermute | solution.py:14
  27.1 3.8 %collective-permute-start.6 = (f32[1,5,5,512]{3,0,2,1:T(1,128)S(1)}, f32[1,5,5,512]{3,0,2,1:T(1,128)S(1)}, u32[]{:S(2)}, u32[]{:S(2)}) collective-permute-start(f32[1,5,5,512]{3,0,2,1:T(1,128)S(1)} %bitcast.781), channel_id=1, source_target_pairs={{0,32},{32,64},{64,96},{96,128},{128,160},{160,192},{192,224},{224... | collective-permute-start | bytes 153608 | tf_op jit(solution)/shard_map/ppermute | solution.py:23
  31.3 1.4 collective-permute-done.6
  34.5 12.5 %while.66 = (s32[]{:T(128)}, f32[5,5,512]{2,1,0:T(8,128)S(1)}, f32[5,11,512]{2,1,0:T(8,128)S(1)}, f32[7,5,5,512]{3,1,2,0:T(8,128)S(1)}, f32[7,5,11,512]{3,2,1,0:...) while((s32[]{:T(128)}, f32[5,5,512]{2,1,0:T(8,128)S(1)}, ...), condition=%wide.region_1.2_spmd, body=%wide.region_0.1_spmd.sunk | while | flops 897537 | bytes 3756661 | solution.py:73
  46.9 1.8 fusion.149
  48.7 1.3 slice.986
  50.0 1.1 slice.987
  51.2 1.3 while.67
  53.3 49.8 %all_gather.15 = f32[16,5,5,512]{3,2,1,0:T(8,128)} all-gather(f32[1,5,5,512]{3,2,1,0:T(8,128)S(1)} %copy-done.23), channel_id=1, replica_groups=mesh['line'=16,'py'=8,'pz'=4] {'line'}, dimensions={0}, use_global_device_ids=true | all-gather | bytes 870400 | tf_op jit(solution)/shard_map/all_gather | solution.py:149
  103.1 5.0 %fusion.148 = (f32[16,5,1,512]{3,2,1,0:T(1,128)S(1)}, f32[16,5,1,512]{3,2,1,0:T(1,128)S(1)}, f32[16,5,1,512]{3,2,1,0:T(1,128)S(1)}, f32[16,5,1,512]{3,2,1,0:T(1,128)S(1)}, f32[16,5,1,512]{3,2,1,0:T(1,128)S(1)}) fusion(f32[16,5,5,512]{3,2,1,0:T(8,128)} %all_gather.15), kind=kLoop, calls=%fused_computation.381 | loop fusion | bytes 1638400 | tf_op jit(solution)/shard_map/slice | solution.py:28
  113.1 35.1 %all_gather.17 = f32[16,5,512]{2,1,0:T(8,128)} all-gather(f32[1,5,512]{2,1,0:T(8,128)S(1)} %copy.112), channel_id=1, replica_groups=mesh['line'=16,'py'=8,'pz'=4] {'line'}, dimensions={0}, use_global_device_ids=true | all-gather | bytes 174080 | tf_op jit(solution)/shard_map/all_gather | solution.py:148
  149.1 34.9 %all_gather.19 = f32[16,5,5,512]{3,2,1,0:T(8,128)S(1)} all-gather(f32[1,5,5,512]{3,2,1,0:T(8,128)S(1)} %get-tuple-element.637), channel_id=1, replica_groups=mesh['line'=16,'py'=8,'pz'=4] {'line'}, dimensions={0}, use_global_device_ids=true | all-gather | bytes 870400 | tf_op jit(solution)/shard_map/all_gather | solution.py:147
  184.0 37.9 %all_gather.18 = f32[16,5,5,512]{3,2,1,0:T(8,128)} all-gather(f32[1,5,5,512]{3,2,1,0:T(8,128)S(1)} %get-tuple-element.638), channel_id=1, replica_groups=mesh['line'=16,'py'=8,'pz'=4] {'line'}, dimensions={0}, use_global_device_ids=true | all-gather | bytes 870400 | tf_op jit(solution)/shard_map/all_gather | solution.py:146
  222.0 1.7 slice-done
  223.7 1.0 copy.145
  227.5 3.6 %add_subtract_fusion = (f32[16,5,5,512]{3,2,1,0:T(8,128)}, f32[16,5,5,512]{3,2,1,0:T(8,128)}) fusion(f32[16,5,5,512]{3,2,1,0:T(8,128)S(1)} %all_gather.19, f32[16,5,512]{2,1,0:T(8,128)S(1)} %copy.118, f32[16,5,512]{2,1,0:T(8,128)S(1)} %copy.117, f32[16,5,512]{2,1,0:T(8,128)S(1)} %copy.116, f32[16,5,512]{2,1,0:T(8,128)S(1)} %copy.115, ...), kind=kLoop, calls=%fused_computation.201 | loop fusion | flops 4096000 | bytes 4915200 | tf_op jit(solution)/shard_map/sub | solution.py:87
  231.1 65.7 %while.68 = (s32[]{:T(128)}, f32[5,5,512]{2,1,0:T(8,128)S(1)}, f32[5,1,512]{2,1,0:T(1,128)S(1)}, f32[16,5,5,512]{3,2,1,0:T(8,128)}, f32[16,5,1,512]{3,2,1,0:T(1,...) while((s32[]{:T(128)}, f32[5,5,512]{2,1,0:T(8,128)S(1)}, ...), condition=%wide.region_5.6_spmd, body=%wide.region_4.5_spmd.sunk | while | flops 385537 | bytes 1909365 | solution.py:73
  232.1 1.0 fusion.175
  236.2 1.0 fusion.175
  240.3 1.0 fusion.175
  244.4 1.0 fusion.175
  252.6 1.0 fusion.175
  265.0 1.0 fusion.175
  281.4 1.0 fusion.175
  296.9 1.4 slice.1038
  298.3 3.2 %while.69 = (s32[]{:T(128)}, f32[5,1,512]{2,1,0:T(1,128)S(1)}, f32[15,5,1,512]{3,0,2,1:T(8,128)S(1)}, f32[15,5,1,512]{3,2,1,0:T(1,128)S(1)}, f32[15,5,5,512]{3,2...) while((s32[]{:T(128)}, f32[5,1,512]{2,1,0:T(1,128)S(1)}, f32[15,5,1,512]{3,0,2,1:T(8,128)S(1)}, ...), condition=%wide.region_7.8_spmd, body=%wide.region_6.7_spmd.sunk | while | flops 25603 | bytes 225389 | solution.py:81
  (1174 shorter events, 84.0 us)
Async XLA Ops:
  6.5 14.3 %copy-start.12 = (f32[8,5,5,4,128]{4,3,2,1,0:T(4,128)S(1)}, f32[8,5,5,4,128]{4,3,2,1,0:T(4,128)}, u32[]{:S(2)}) copy-start(f32[8,5,5,4,128]{4,3,2,1,0:T(4,128)} %param.16) | copy-start | bytes 1228804
  6.5 19.6 %slice-start.2 = ((f32[8,5,5,4,128]{4,3,2,1,0:T(4,128)}), f32[7,5,5,4,128]{4,3,2,1,0:T(4,128)S(1)}, s32[]{:S(2)}) async-start(f32[8,5,5,4,128]{4,3,2,1,0:T(4,128)} %param.16), calls=%async_computation.3 | async-start | bytes 716800 | tf_op jit(solution)/shard_map/slice | solution.py:98
  6.5 215.4 %all-gather.2.cloned.1.call-start = ((), (), s32[]{:S(2)}) async-start(), calls=%async_computation | async-start | bytes 2785280 | tf_op jit(solution)/shard_map/all_gather | solution.py:150
  7.7 13.9 %collective-permute-start.4 = (f32[8,5,4,1]{3,2,1,0:T(4,128)S(1)}, f32[8,5,4,1]{3,2,1,0:T(4,128)S(1)}, u32[]{:S(2)}, u32[]{:S(2)}) collective-permute-start(f32[8,5,4,1]{3,2,1,0:T(4,128)S(1)} %get-tuple-element.646), channel_id=1, source_target_pairs={{1,0},{2,1},{3,2},{5,4},{6,5},{7,6},{9,8},{10,9},{11,10},{13,12},{... | collective-permute-start | bytes 1928 | tf_op jit(solution)/shard_map/ppermute | solution.py:15
  9.0 18.1 %collective-permute-start.5 = (f32[8,5,4,1]{3,2,1,0:T(4,128)S(1)}, f32[8,5,4,1]{3,2,1,0:T(4,128)S(1)}, u32[]{:S(2)}, u32[]{:S(2)}) collective-permute-start(f32[8,5,4,1]{3,2,1,0:T(4,128)S(1)} %get-tuple-element.647), channel_id=1, source_target_pairs={{0,1},{1,2},{2,3},{4,5},{5,6},{6,7},{8,9},{9,10},{10,11},{12,13},{... | collective-permute-start | bytes 1928 | tf_op jit(solution)/shard_map/ppermute | solution.py:14
  13.6 17.3 %collective-permute-start.2 = (f32[8,5,1,128]{3,2,1,0:T(1,128)S(1)}, f32[8,5,1,128]{3,2,1,0:T(1,128)S(1)}, u32[]{:S(2)}, u32[]{:S(2)}) collective-permute-start(f32[8,5,1,128]{3,2,1,0:T(1,128)S(1)} %get-tuple-element.644), channel_id=1, source_target_pairs={{4,0},{8,4},{12,8},{16,12},{20,16},{24,20},{28,24},{5,1},{9,5},{13... | collective-permute-start | bytes 61448 | tf_op jit(solution)/shard_map/ppermute | solution.py:15
  15.5 15.4 %collective-permute-start.3 = (f32[8,5,1,128]{3,2,1,0:T(1,128)S(1)}, f32[8,5,1,128]{3,2,1,0:T(1,128)S(1)}, u32[]{:S(2)}, u32[]{:S(2)}) collective-permute-start(f32[8,5,1,128]{3,2,1,0:T(1,128)S(1)} %get-tuple-element.645), channel_id=1, source_target_pairs={{0,4},{4,8},{8,12},{12,16},{16,20},{20,24},{24,28},{1,5},{5,9},{9,... | collective-permute-start | bytes 61448 | tf_op jit(solution)/shard_map/ppermute | solution.py:14
  18.7 12.2 %collective-permute-start = (f32[1,5,4,128]{3,2,1,0:T(4,128)S(1)}, f32[1,5,4,128]{3,2,1,0:T(4,128)S(1)}, u32[]{:S(2)}, u32[]{:S(2)}) collective-permute-start(f32[1,5,4,128]{3,2,1,0:T(4,128)S(1)} %get-tuple-element.615), channel_id=1, source_target_pairs={{32,0},{64,32},{96,64},{128,96},{160,128},{192,160},{224,192},{256... | collective-permute-start | bytes 30728 | tf_op jit(solution)/shard_map/ppermute | solution.py:15
  20.9 5.6 %copy-start = (f32[8,5,5,512]{3,2,1,0:T(8,128)}, f32[8,5,5,512]{3,2,1,0:T(8,128)S(1)}, u32[]{:S(2)}) copy-start(f32[8,5,5,512]{3,2,1,0:T(8,128)S(1)} %broadcast_multiply_fusion.6) | copy-start | bytes 1228804
  21.6 9.4 %collective-permute-start.1 = (f32[1,5,4,128]{3,2,1,0:T(4,128)S(1)}, f32[1,5,4,128]{3,2,1,0:T(4,128)S(1)}, u32[]{:S(2)}, u32[]{:S(2)}) collective-permute-start(f32[1,5,4,128]{3,2,1,0:T(4,128)S(1)} %get-tuple-element.616), channel_id=1, source_target_pairs={{0,32},{32,64},{64,96},{96,128},{128,160},{160,192},{192,224},{224... | collective-permute-start | bytes 30728 | tf_op jit(solution)/shard_map/ppermute | solution.py:14
  26.4 7.0 %copy-start.27 = (pred[7]{0:T(512)(128)(4,1)S(1)}, pred[7]{0:T(512)(128)(4,1)}, u32[]{:S(2)}) copy-start(pred[7]{0:T(512)(128)(4,1)} %constant.197.clone.1) | copy-start | bytes 25
  27.1 5.6 %collective-permute-start.6 = (f32[1,5,5,512]{3,0,2,1:T(1,128)S(1)}, f32[1,5,5,512]{3,0,2,1:T(1,128)S(1)}, u32[]{:S(2)}, u32[]{:S(2)}) collective-permute-start(f32[1,5,5,512]{3,0,2,1:T(1,128)S(1)} %bitcast.781), channel_id=1, source_target_pairs={{0,32},{32,64},{64,96},{96,128},{128,160},{160,192},{192,224},{224... | collective-permute-start | bytes 153608 | tf_op jit(solution)/shard_map/ppermute | solution.py:23
  31.2 80.2 %copy-start.22 = (f32[8,5,4,128]{3,2,1,0:T(4,128)}, f32[8,5,4,128]{3,2,1,0:T(4,128)S(1)}, u32[]{:S(2)}) copy-start(f32[8,5,4,128]{3,2,1,0:T(4,128)S(1)} %fusion.121) | copy-start | bytes 245764
  31.2 2.3 copy-start.24
  46.9 3.1 copy-start.21
  51.2 2.1 copy-start.23
  108.1 3.7 %copy-start.4 = (f32[16,5,1,512]{3,2,1,0:T(1,128)}, f32[16,5,1,512]{3,2,1,0:T(1,128)S(1)}, u32[]{:S(2)}) copy-start(f32[16,5,1,512]{3,2,1,0:T(1,128)S(1)} %get-tuple-element.590) | copy-start | bytes 491524
  108.1 3.7 %copy-start.6 = (f32[16,5,1,512]{3,2,1,0:T(1,128)}, f32[16,5,1,512]{3,2,1,0:T(1,128)S(1)}, u32[]{:S(2)}) copy-start(f32[16,5,1,512]{3,2,1,0:T(1,128)S(1)} %get-tuple-element.591) | copy-start | bytes 491524
  108.1 3.7 %copy-start.8 = (f32[16,5,1,512]{3,2,1,0:T(1,128)}, f32[16,5,1,512]{3,2,1,0:T(1,128)S(1)}, u32[]{:S(2)}) copy-start(f32[16,5,1,512]{3,2,1,0:T(1,128)S(1)} %get-tuple-element.592) | copy-start | bytes 491524
  108.1 3.7 %copy-start.10 = (f32[16,5,1,512]{3,2,1,0:T(1,128)}, f32[16,5,1,512]{3,2,1,0:T(1,128)S(1)}, u32[]{:S(2)}) copy-start(f32[16,5,1,512]{3,2,1,0:T(1,128)S(1)} %get-tuple-element.593) | copy-start | bytes 491524
  110.4 1.4 copy-start.26
  111.4 1.5 slice-start.3
  111.4 1.6 copy-start.19
  111.8 37.2 %copy-start.1 = (f32[8,5,5,512]{3,2,1,0:T(8,128)S(1)}, f32[8,5,5,512]{3,2,1,0:T(8,128)}, u32[]{:S(2)}) copy-start(f32[8,5,5,512]{3,2,1,0:T(8,128)} %copy-done) | copy-start | bytes 1228804
  222.0 1.7 slice-start
  225.4 1.3 copy-start.18
  225.7 1.8 copy-start.13
  225.7 1.8 copy-start.14
  225.7 1.7 copy-start.15
  225.7 1.7 copy-start.16
  225.8 1.7 copy-start.17
  227.5 3.6 %copy-start.20 = (f32[16,5,1,512]{3,2,1,0:T(1,128)S(1)}, f32[16,5,1,512]{3,2,1,0:T(1,128)}, u32[]{:S(2)}) copy-start(f32[16,5,1,512]{3,2,1,0:T(1,128)} %custom-call.5) | copy-start | bytes 491524
  (8 other events, 7.6 us)
Sparse Core Ops, SparseCore 0:
  53.4 81.9 all-gather.1
where the time goes:
time: 314 us; the launch traced here: 309 us
  blocking collectives  158 us (50%)
  local copies, waits for them, and re-layouts  64 us (20%)
  other arithmetic  44.5 us (14%)
  starting transfers between devices  19.8 us (6%)
  between operations  14.3 us (5%)
  loops' own time  7.82 us (2%)
    all_gather x1, blocking collectives, per_device(): lax.all_gather(sep_upper[None], 'line', axis=0, tiled=True)  49.8 us
    all_gather x1, blocking collectives, per_device(): lax.all_gather(own_lower[None], 'line', axis=0, tiled=True)  37.9 us
    all_gather x1, blocking collectives, per_device(): lax.all_gather(own_right[None], 'line', axis=0, tiled=True)  35.1 us
    all_gather x1, blocking collectives, per_device(): lax.all_gather(own_diag[None], 'line', axis=0, tiled=True)  34.9 us
    dynamic_update_slice x46, local copies, waits for them, and re-layouts, block_thomas(): lax.scan(forward, start_state, (lower, diagonal, upper, right))  15.9 us
    slice x16, other arithmetic, mat_mul(): total = left_mat[..., :, 0:1, :] * right_mat[..., 0:1, :, :]  15.3 us
    sub x23, other arithmetic, forward(): pivot_mat = diag_row - mat_mul(lower_row, prev_upper)  15.2 us
    squeeze x16, local copies, waits for them, and re-layouts, block_thomas(): lax.scan(forward, start_state, (lower, diagonal, upper, right))  15.1 us
  transfers between devices with their start and end apart: 8, of which 1 were waited for; matrix products, arithmetic and copies ran while one was open for 4% of the time, Pallas kernels for 0%

commit v1 on v0

v1 whole, which is shorter than its diff:
```python
import functools

import jax
import jax.numpy as jnp
from jax import lax
from jax.experimental import pallas as pl
from jax.experimental.pallas import tpu as pltpu
from jax.sharding import PartitionSpec as P

MESH = pl.DeviceIdType.MESH
B = 5
SYM = [(i, j) for i in range(B) for j in range(i, B)]
POS = {}
for _n, (_i, _j) in enumerate(SYM):
    POS[_i, _j] = POS[_j, _i] = _n
NSYM = len(SYM)
GL, GR, CC = 0, NSYM, 2 * NSYM
NMAT = 2 * NSYM + B * B
MROWS = 56
GROWS = 16


def total(terms):
    result = terms[0]
    for term in terms[1:]:
        result = result + term
    return result


def sym_inverse(a):
    a = list(a)
    for k in range(B):
        scaling = 1.0 / a[POS[k, k]]
        col = {i: a[POS[i, k]] for i in range(B) if i != k}
        scaled = {i: col[i] * scaling for i in col}
        for i, j in SYM:
            if i != k and j != k:
                a[POS[i, j]] = a[POS[i, j]] - scaled[i] * col[j]
        for i in col:
            a[POS[i, k]] = scaled[i]
        a[POS[k, k]] = -scaling
    return [-entry for entry in a]


def sym_times(inv, mat):
    return [[total([inv[POS[i, k]] * mat[k][j] for k in range(B)]) for j in range(B)] for i in range(B)]


def mat_vec(mat, vec):
    return [total([mat[i][k] * vec[k] for k in range(B)]) for i in range(B)]


def sym_vec(mat, vec):
    return [total([mat[POS[i, k]] * vec[k] for k in range(B)]) for i in range(B)]


def transposed(mat):
    return [[mat[j][i] for j in range(B)] for i in range(B)]


def product_sym(left, right):
    return [total([left[i][k] * right[k][j] for k in range(B)]) for i, j in SYM]


def product(left, right):
    return [[total([left[i][k] * right[k][j] for k in range(B)]) for j in range(B)] for i in range(B)]


def as_mat(flat):
    return [[flat[i * B + j] for j in range(B)] for i in range(B)]


def kernel(
    n,
    npy,
    npz,
    flux_hbm,
    jac_hbm,
    diss_hbm,
    out_ref,
    fv,
    jv,
    dv,
    xl,
    xr,
    yl,
    yr,
    zl,
    zr,
    ysl,
    ysr,
    zsl,
    zsr,
    rv,
    el,
    facs,
    gel,
    yv,
    msend,
    mrecv,
    gsend,
    grecv,
    sfac,
    sol,
    xrecv,
    lsem,
    hsend,
    hrecv,
    m_s,
    m_r,
    g_s,
    g_r,
    x_s,
    x_r,
):
    p = lax.axis_index("line")
    py = lax.axis_index("py")
    pz = lax.axis_index("pz")
    core = lax.rem(py, 2)
    ncell = jv.shape[0] // (B * B)
    solver = [4 * s + 2 * core for s in range(4)]
    is_solver = lax.rem(p + n - 2 * core, 4) == 0
    mine = lax.div(p, 4)

    barrier = pltpu.get_barrier_semaphore()
    peers = [{"line": lax.rem(p + o, n)} for o in range(1, n)]
    peers += [{"py": lax.rem(py + o, npy)} for o in (1, npy - 1)]
    peers += [{"pz": lax.rem(pz + o, npz)} for o in (1, npz - 1)]
    for peer in peers:
        pl.semaphore_signal(barrier, inc=1, device_id=peer, device_id_type=MESH)

    loads = [
        pltpu.make_async_copy(flux_hbm, fv, lsem.at[0]),
        pltpu.make_async_copy(jac_hbm, jv, lsem.at[1]),
        pltpu.make_async_copy(diss_hbm, dv, lsem.at[2]),
    ]
    for load in loads:
        load.start()
    sol[...] = jnp.zeros_like(sol)
    msend[...] = jnp.zeros_like(msend)
    gsend[...] = jnp.zeros_like(gsend)
    ncomp = ncell * B
    shape = (4, 128)
    row = lax.broadcasted_iota(jnp.int32, shape, 0)
    lane = lax.broadcasted_iota(jnp.int32, shape, 1)
    zero = jnp.zeros(shape, jnp.float32)
    loads[0].wait()

    packed_l, packed_r = zero, zero
    for k in range(ncomp):
        cell = k // B
        f_after = fv[0, k + B] if cell < ncell - 1 else zero
        f_before = fv[0, k - B] if cell > 0 else zero
        g = fv[1, k]
        h = fv[2, k]
        blank = jnp.zeros((1, 128), jnp.float32)
        dy = jnp.concatenate([g[1:], blank], 0) - jnp.concatenate([blank, g[:-1]], 0)
        h_after = jnp.where(lane == 127, 0.0, pltpu.roll(h, 127, 1))
        h_before = jnp.where(lane == 0, 0.0, pltpu.roll(h, 1, 1))
        rv[k] = -0.5 * ((f_after - f_before) + dy + (h_after - h_before))
        ysl[k : k + 1, :] = g[0:1]
        ysr[k : k + 1, :] = g[3:4]
        packed_l = jnp.where(lane == k, pltpu.roll(h, k, 1), packed_l)
        packed_r = jnp.where(lane == k, pltpu.roll(h, (k + 1) % 128, 1), packed_r)
    zsl[...] = packed_l
    zsr[...] = packed_r

    loads[1].wait()
    loads[2].wait()

    def first_level(j, carry):
        m = 2 * j + 1
        cut = jnp.logical_and(m == ncell - 1, p == n - 1)
        keep = jnp.where(cut, 0.0, 1.0)
        before = [jv[(m - 1) * B * B + i * B + k] for i, k in SYM]
        after = [jv[m * B * B + i * B + k] * keep for i, k in SYM]
        inv = 1.0 / (1.0 + dv[m])
        full_b = [[before[POS[i, k]] for k in range(B)] for i in range(B)]
        full_a = [[after[POS[i, k]] for k in range(B)] for i in range(B)]
        scaled_b = [[(before[POS[i, k]] * inv) for k in range(B)] for i in range(B)]
        scaled_a = [[(after[POS[i, k]] * inv) for k in range(B)] for i in range(B)]
        for e, value in enumerate(product_sym(full_b, scaled_b)):
            el[j * NMAT + GL + e] = value
        for e, value in enumerate(product_sym(full_a, scaled_a)):
            el[j * NMAT + GR + e] = value
        couple = product(full_a, scaled_b)
        for e in range(B * B):
            el[j * NMAT + CC + e] = couple[e // B][e % B]
        return carry

    lax.fori_loop(0, ncell // 2, first_level, 0)

    def merge(i, carry):
        a, b, new = 2 * i * NMAT, (2 * i + 1) * NMAT, (4 + i) * NMAT
        m = jnp.where(i == 2, 4, 2 + 4 * i)
        pivot = [el[a + GR + e] + el[b + GL + e] for e in range(NSYM)]
        diag = 1.0 + dv[m]
        for k in range(B):
            pivot[POS[k, k]] = pivot[POS[k, k]] + diag
        inv = sym_inverse(pivot)
        ca = as_mat([el[a + CC + e] for e in range(B * B)])
        cb = as_mat([el[b + CC + e] for e in range(B * B)])
        w = sym_times(inv, ca)
        u = sym_times(inv, transposed(cb))
        gl_new = product_sym(transposed(ca), w)
        gr_new = product_sym(cb, u)
        c_new = product(cb, w)
        for e in range(NSYM):
            el[new + GL + e] = el[a + GL + e] - gl_new[e]
            el[new + GR + e] = el[b + GR + e] - gr_new[e]
            facs[i * 65 + e] = inv[e]
        for e in range(B * B):
            el[new + CC + e] = c_new[e // B][e % B]
            facs[i * 65 + NSYM + e] = w[e // B][e % B]
            facs[i * 65 + NSYM + B * B + e] = u[e // B][e % B]
        return carry

    lax.fori_loop(0, 3, merge, 0)

    diag0 = 1.0 + dv[0]
    for e in range(NMAT):
        value = el[6 * NMAT + e]
        if e < NSYM and SYM[e][0] == SYM[e][1]:
            value = value + diag0
        msend[pl.ds(e, 4, stride=MROWS), :] = value

    pl.semaphore_wait(barrier, len(peers))

    halo = []

    def send_halo(src, dst, index, peer):
        copy = pltpu.make_async_remote_copy(
            src_ref=src,
            dst_ref=dst,
            send_sem=hsend.at[index],
            recv_sem=hrecv.at[index],
            device_id=peer,
            device_id_type=MESH,
        )
        copy.start()
        halo.append(copy)

    send_halo(fv.at[0, pl.ds(ncomp - B, B)], xl, 0, {"line": lax.rem(p + 1, n)})
    send_halo(fv.at[0, pl.ds(0, B)], xr, 1, {"line": lax.rem(p + n - 1, n)})
    send_halo(ysr, yl, 2, {"py": lax.rem(py + 1, npy)})
    send_halo(ysl, yr, 3, {"py": lax.rem(py + npy - 1, npy)})
    send_halo(zsr, zl, 4, {"pz": lax.rem(pz + 1, npz)})
    send_halo(zsl, zr, 5, {"pz": lax.rem(pz + npz - 1, npz)})

    def part_copies(src, dst, rows, send_sem, recv_sem, s):
        here = src.at[pl.ds(s * rows, rows)]
        there = dst.at[pl.ds(pl.multiple_of(p * rows, 8), rows)]
        away = pltpu.make_async_remote_copy(
            src_ref=here,
            dst_ref=there,
            send_sem=send_sem.at[s],
            recv_sem=recv_sem.at[p],
            device_id={"line": solver[s]},
            device_id_type=MESH,
        )
        return away, pltpu.make_async_copy(here, there, send_sem.at[s])

    def start_parts(src, dst, rows, send_sem, recv_sem):
        for s in range(4):
            away, near = part_copies(src, dst, rows, send_sem, recv_sem, s)
            pl.when(solver[s] != p)(away.start)
            pl.when(solver[s] == p)(near.start)

    def finish_parts(src, dst, rows, send_sem, recv_sem):
        for s in range(4):
            away, near = part_copies(src, dst, rows, send_sem, recv_sem, s)
            pl.when(solver[s] != p)(away.wait_send)
            pl.when(solver[s] == p)(near.wait)

    def await_parts(src, dst, rows, send_sem, recv_sem):
        def one(q, carry):
            copy = pltpu.make_async_remote_copy(
                src_ref=src.at[pl.ds(0, rows)],
                dst_ref=dst.at[pl.ds(pl.multiple_of(q * rows, 8), rows)],
                send_sem=send_sem.at[0],
                recv_sem=recv_sem.at[q],
                device_id={"line": solver[0]},
                device_id_type=MESH,
            )
            pl.when(q != p)(copy.wait_recv)
            return carry

        lax.fori_loop(0, n, one, 0)

    mats = (msend, mrecv, MROWS, m_s, m_r)
    sides = (gsend, grecv, GROWS, g_s, g_r)
    start_parts(*mats)

    for copy in halo:
        copy.wait_recv()

    x_first = jnp.where(p > 0, 0.5, 0.0)
    x_last = jnp.where(p < n - 1, -0.5, 0.0)
    y_first = jnp.where(row == 0, jnp.where(py > 0, 0.5, 0.0), 0.0)
    y_last = jnp.where(row == 3, jnp.where(py < npy - 1, -0.5, 0.0), 0.0)
    z_first = jnp.where(lane == 0, jnp.where(pz > 0, 0.5, 0.0), 0.0)
    z_last = jnp.where(lane == 127, jnp.where(pz < npz - 1, -0.5, 0.0), 0.0)
    z_left, z_right = zl[...], zr[...]
    for k in range(ncomp):
        value = rv[k] + y_first * yl[k : k + 1, :] + y_last * yr[k : k + 1, :]
        value = value + z_first * pltpu.roll(z_left, (128 - k) % 128, 1)
        value = value + z_last * pltpu.roll(z_right, 127 - k, 1)
        if k < B:
            value = value + x_first * xl[k]
        if k >= ncomp - B:
            value = value + x_last * xr[k - ncomp + B]
        rv[k] = value

    def sym_face(f):
        return [jv[f * B * B + i * B + k] for i, k in SYM]

    keep_last = jnp.where(p == n - 1, 0.0, 1.0)
    g_left, g_right = [None] * 7, [None] * 7
    for j in range(ncell // 2):
        m = 2 * j + 1
        inv = 1.0 / (1.0 + dv[m])
        scaled = [rv[m * B + i] * inv for i in range(B)]
        g_left[j] = [-v for v in sym_vec(sym_face(m - 1), scaled)]
        after = scaled if m < ncell - 1 else [v * keep_last for v in scaled]
        g_right[j] = sym_vec(sym_face(m), after)
    for i, m in enumerate((2, 6, 4)):
        a, b = 2 * i, 2 * i + 1
        q = [rv[m * B + c] + g_right[a][c] + g_left[b][c] for c in range(B)]
        w = as_mat([facs[i * 65 + NSYM + e] for e in range(B * B)])
        u = as_mat([facs[i * 65 + NSYM + B * B + e] for e in range(B * B)])
        more_l = mat_vec(transposed(w), q)
        more_r = mat_vec(transposed(u), q)
        g_left[4 + i] = [g_left[a][c] + more_l[c] for c in range(B)]
        g_right[4 + i] = [g_right[b][c] + more_r[c] for c in range(B)]
        for c in range(B):
            gel[i * B + c] = q[c]
    for c in range(B):
        gsend[pl.ds(c, 4, stride=GROWS), :] = rv[c] + g_left[6][c]
        gsend[pl.ds(B + c, 4, stride=GROWS), :] = g_right[6][c]

    start_parts(*sides)
    for i in range(3):
        value = sym_vec([facs[i * 65 + e] for e in range(NSYM)], [gel[i * B + c] for c in range(B)])
        for c in range(B):
            yv[i * B + c] = value[c]

    def answer_copy(q):
        return pltpu.make_async_remote_copy(
            src_ref=sol.at[pl.ds(pl.multiple_of(q * 8, 8), 16)],
            dst_ref=xrecv.at[pl.ds(pl.multiple_of(mine * 16, 16), 16)],
            send_sem=x_s.at[q],
            recv_sem=x_r.at[mine],
            device_id={"line": q},
            device_id_type=MESH,
        )

    own_answer = pltpu.make_async_copy(
        sol.at[pl.ds(pl.multiple_of(p * 8, 8), 16)],
        xrecv.at[pl.ds(pl.multiple_of(mine * 16, 16), 16)],
        x_s.at[p],
    )

    def solve():
        finish_parts(*mats)
        await_parts(*mats)

        def even(e):
            return mrecv[pl.ds(e, 8, stride=2 * MROWS), :]

        def odd(e):
            return mrecv[pl.ds(MROWS + e, 8, stride=2 * MROWS), :]

        inv0 = sym_inverse([odd(GL + e) + even(GR + e) for e in range(NSYM)])
        ca = as_mat([even(CC + e) for e in range(B * B)])
        cb = as_mat([odd(CC + e) for e in range(B * B)])
        w0 = sym_times(inv0, ca)
        u0 = sym_times(inv0, transposed(cb))
        less_l = product_sym(transposed(ca), w0)
        less_r = product_sym(cb, u0)
        diag = [even(GL + e) - less_l[e] + pltpu.roll(odd(GR + e) - less_r[e], 1, 0) for e in range(NSYM)]
        couple = product(cb, w0)
        base = 0

        def keep(values):
            nonlocal base
            start = base
            for value in values:
                sfac[base] = value
                base += 1
            return start

        def flat(mat):
            return [entry for line in mat for entry in line]

        at_inv0, at_w0, at_u0 = keep(inv0), keep(flat(w0)), keep(flat(u0))
        levels = []
        for step in (1, 2, 4):
            inv = sym_inverse(diag)
            left = [[pltpu.roll(entry, step, 0) for entry in line] for line in couple]
            w = sym_times(inv, left)
            u = sym_times(inv, transposed(couple))
            levels.append((step, keep(flat(w)), keep(flat(u))))
            less_l = product_sym(transposed(left), w)
            less_r = product_sym(couple, u)
            diag = [
                diag[e] - pltpu.roll(less_l[e], 8 - step, 0) - pltpu.roll(less_r[e], step, 0)
                for e in range(NSYM)
            ]
            if step < 4:
                couple = [[pltpu.roll(v, 8 - step, 0) for v in line] for line in product(couple, w)]
        at_last = keep(sym_inverse(diag))

        finish_parts(*sides)
        await_parts(*sides)

        def saved(start, count):
            return [sfac[start + e] for e in range(count)]

        def even_side(e):
            return grecv[pl.ds(e, 8, stride=2 * GROWS), :]

        def odd_side(e):
            return grecv[pl.ds(GROWS + e, 8, stride=2 * GROWS), :]

        w0 = as_mat(saved(at_w0, B * B))
        u0 = as_mat(saved(at_u0, B * B))
        q = [odd_side(c) + even_side(B + c) for c in range(B)]
        more_l = mat_vec(transposed(w0), q)
        more_r = mat_vec(transposed(u0), q)
        side = [
            even_side(c) + more_l[c] + pltpu.roll(odd_side(B + c) + more_r[c], 1, 0) for c in range(B)
        ]
        for step, at_w, at_u in levels:
            more_l = mat_vec(transposed(as_mat(saved(at_w, B * B))), side)
            more_r = mat_vec(transposed(as_mat(saved(at_u, B * B))), side)
            side = [
                side[c] + pltpu.roll(more_l[c], 8 - step, 0) + pltpu.roll(more_r[c], step, 0)
                for c in range(B)
            ]
        x_even = sym_vec(saved(at_last, NSYM), side)
        x_next = [pltpu.roll(v, 7, 0) for v in x_even]
        own = sym_vec(saved(at_inv0, NSYM), q)
        from_l = mat_vec(w0, x_even)
        from_r = mat_vec(u0, x_next)
        for c in range(B):
            sol[pl.ds(c, 8, stride=16), :] = x_even[c]
            sol[pl.ds(8 + c, 8, stride=16), :] = own[c] + from_l[c] + from_r[c]

        def send_one(q, carry):
            pl.when(q != p)(answer_copy(q).start)
            return carry

        lax.fori_loop(0, n, send_one, 0)
        own_answer.start()
        own_answer.wait()

    pl.when(is_solver)(solve)

    for s in range(4):
        copy = pltpu.make_async_remote_copy(
            src_ref=sol.at[pl.ds(0, 16)],
            dst_ref=xrecv.at[pl.ds(s * 16, 16)],
            send_sem=x_s.at[0],
            recv_sem=x_r.at[s],
            device_id={"line": solver[s]},
            device_id_type=MESH,
        )
        pl.when(solver[s] != p)(copy.wait_recv)

    x = [None] * (ncell + 1)
    x[0] = [xrecv[pl.ds(c, 4, stride=16), :] for c in range(B)]
    x[ncell] = [xrecv[pl.ds(8 + c, 4, stride=16), :] for c in range(B)]
    for i, (m, a, b) in ((2, (4, 0, 8)), (0, (2, 0, 4)), (1, (6, 4, 8))):
        w = as_mat([facs[i * 65 + NSYM + e] for e in range(B * B)])
        u = as_mat([facs[i * 65 + NSYM + B * B + e] for e in range(B * B)])
        from_l, from_r = mat_vec(w, x[a]), mat_vec(u, x[b])
        x[m] = [yv[i * B + c] + from_l[c] + from_r[c] for c in range(B)]
    for m in range(1, ncell, 2):
        inv = 1.0 / (1.0 + dv[m])
        from_l = sym_vec(sym_face(m - 1), x[m - 1])
        after = x[m + 1] if m < ncell - 1 else [v * keep_last for v in x[m + 1]]
        from_r = sym_vec(sym_face(m), after)
        x[m] = [(rv[m * B + c] + from_l[c] - from_r[c]) * inv for c in range(B)]
    for m in range(ncell):
        for c in range(B):
            out_ref[m * B + c] = x[m][c]

    for copy in halo:
        copy.wait_send()

    def others():
        finish_parts(*mats)
        finish_parts(*sides)

    pl.when(jnp.logical_not(is_solver))(others)

    def answers_sent():
        def one(q, carry):
            pl.when(q != p)(answer_copy(q).wait_send)
            return carry

        lax.fori_loop(0, n, one, 0)

    pl.when(is_solver)(answers_sent)


def per_device(sizes, fluxes, jacobian, dissipation):
    n, npy, npz = sizes
    ncell = jacobian.shape[0]
    tail = jacobian.shape[3:]
    f32 = jnp.float32
    vmem, dma = pltpu.VMEM, pltpu.SemaphoreType.DMA
    tile = lambda count: vmem((count,) + tail, f32)
    flat = lambda rows: vmem((rows, 128), f32)
    ncomp = ncell * B
    out = pl.pallas_call(
        functools.partial(kernel, n, npy, npz),
        out_shape=jax.ShapeDtypeStruct((ncomp,) + tail, f32),
        in_specs=[pl.BlockSpec(memory_space=pl.ANY)] * 3,
        out_specs=pl.BlockSpec(memory_space=pltpu.VMEM),
        scratch_shapes=[
            vmem((3, ncomp) + tail, f32),
            tile(ncell * B * B),
            tile(ncell),
            tile(B),
            tile(B),
            flat(ncomp),
            flat(ncomp),
            vmem(tail, f32),
            vmem(tail, f32),
            flat(ncomp),
            flat(ncomp),
            vmem(tail, f32),
            vmem(tail, f32),
            tile(ncomp),
            tile(7 * NMAT),
            tile(3 * 65),
            tile(3 * B),
            tile(3 * B),
            flat(4 * MROWS),
            flat(n * MROWS),
            flat(4 * GROWS),
            flat(n * GROWS),
            vmem((256, 8, 128), f32),
            flat((n + 1) * 8),
            flat(4 * 16),
            dma((3,)),
            dma((6,)),
            dma((6,)),
            dma((4,)),
            dma((n,)),
            dma((4,)),
            dma((n,)),
            dma((n,)),
            dma((4,)),
        ],
        compiler_params=pltpu.CompilerParams(
            collective_id=0, has_side_effects=True, vmem_limit_bytes=32 * 1024 * 1024
        ),
    )(
        fluxes.reshape((3, ncomp) + tail),
        jacobian.reshape((ncell * B * B,) + tail),
        dissipation,
    )
    return out.reshape((ncell, B) + tail)


def solution(mesh):
    sizes = tuple(mesh.shape[name] for name in ("line", "py", "pz"))
    return jax.shard_map(
        functools.partial(per_device, sizes),
        mesh=mesh,
        in_specs=(
            P(None, "line", None, "py", "pz"),
            P("line", None, None, "py", "pz"),
            P("line", "py", "pz"),
        ),
        out_specs=P("line", None, "py", "pz"),
        check_vma=False,
    )
```

time: 314 us -> 39.9 us (0.13); the launches traced: 309 us -> 39.5 us
  blocking collectives: 158 us -> 0 us
  local copies, waits for them, and re-layouts: 64 us -> 3.3 us
  other arithmetic: 44.5 us -> 0 us
  Pallas kernels: 0 us -> 36.2 us
  starting transfers between devices: 19.8 us -> 0 us
  between operations: 14.3 us -> 0.01 us
  loops' own time: 7.82 us -> 0 us
    all_gather x4 -> x0, blocking collectives: 158 us -> none  [the longest x1 49.8 us: per_device(): lax.all_gather(sep_upper[None], 'line', axis=0, tiled=True)]
    pallas_call x0 -> x1, Pallas kernels: none -> 36.2 us  [per_device(): pl.pallas_call(functools.partial(kernel, n, npy, npz), out_shape=jax.Shap...]
    sub x193 -> x0, other arithmetic: 22.4 us -> none  [the longest x23 15.2 us: forward(): pivot_mat = diag_row - mat_mul(lower_row, prev_upper)]
    ppermute x7 -> x0, starting transfers between devices: 19.8 us -> none  [the longest x3 11.5 us: padded_2(): before = lax.ppermute(last, axis, up)]
    slice x340 -> x0, local copies, waits for them, and re-layouts: 18 us -> none  [the longest x33 5.16 us: mat_mul(): total = left_mat[..., :, 0:1, :] * right_mat[..., 0:1, :, :]]
    dynamic_update_slice x61 -> x0, local copies, waits for them, and re-layouts: 17.3 us -> none  [the longest x46 15.9 us: block_thomas(): lax.scan(forward, start_state, (lower, diagonal, upper, right))]
    squeeze x40 -> x0, local copies, waits for them, and re-layouts: 16.4 us -> none  [the longest x16 15.1 us: block_thomas(): lax.scan(forward, start_state, (lower, diagonal, upper, right))]
    slice x64 -> x0, other arithmetic: 16.4 us -> none  [the longest x16 15.3 us: mat_mul(): total = left_mat[..., :, 0:1, :] * right_mat[..., 0:1, :, :]]
  transfers between devices with their start and end apart: 8 -> 0, of which waited for: 1 -> 0; matrix products, arithmetic and copies ran while one was open for 4% -> 0% of each run, Pallas kernels for 0% -> 0%
where the time goes in v1:
time: 39.9 us; the launch traced here: 39.5 us
  Pallas kernels  36.2 us (91%)
  local copies, waits for them, and re-layouts  3.3 us (8%)
    pallas_call x1, Pallas kernels, per_device(): pl.pallas_call(functools.partial(kernel, n, npy, npz), out_shape=jax.Shap...  36.2 us
    unnamed x7, local copies, waits for them, and re-layouts  3.3 us

profile of v1, /device:TPU:24, one launch (start us, length us, event | category | flops | bytes accessed | tf_op | source)
XLA Modules:
  0.0 39.5 jit_solution(15200969800859167670)
XLA Ops:
  0.0 0.0 copy-start
  0.0 1.0 %copy-done = f32[8,5,5,4,128]{4,3,2,1,0:T(4,128)S(1)} copy-done((f32[8,5,5,4,128]{4,3,2,1,0:T(4,128)S(1)}, f32[8,5,5,4,128]{4,3,2,1,0:T(4,128)}, u32[]{:S(2)}) %copy-start) | copy-done | bytes 409624
  1.0 0.0 copy-start.1
  1.0 0.9 %copy-done.1 = f32[3,8,5,4,128]{4,3,2,1,0:T(4,128)S(1)} copy-done((f32[3,8,5,4,128]{4,3,2,1,0:T(4,128)S(1)}, f32[3,8,5,4,128]{4,3,2,1,0:T(4,128)}, u32[]{:S(2)}) %copy-start.1) | copy-done | bytes 245784
  1.9 0.0 copy-start.2
  1.9 0.7 %copy-done.2 = f32[8,4,128]{2,1,0:T(4,128)S(1)} copy-done((f32[8,4,128]{2,1,0:T(4,128)S(1)}, f32[8,4,128]{2,1,0:T(4,128)}, u32[]{:S(2)}) %copy-start.2) | copy-done | bytes 16408
  2.7 36.2 %shard_map.37 = f32[40,4,128]{2,1,0:T(4,128)S(1)} custom-call(f32[3,40,4,128]{3,2,1,0:T(4,128)S(1)} %bitcast.5, f32[200,4,128]{2,1,0:T(4,128)S(1)} %bitcast.3, f32[8,4,128]{2,1,0:T(4,128)S(1)} %copy-done.2), custom_call_target="tpu_custom_call" | custom-call | tf_op jit(solution)/shard_map/pallas_call | solution.py:516
  38.8 0.6 %copy.5 = f32[8,5,4,128]{3,2,1,0:T(4,128)} copy(f32[8,5,4,128]{3,2,1,0:T(4,128)S(1)} %bitcast.4) | data formatting | bytes 163840
Async XLA Ops:
  0.0 1.0 %copy-start = (f32[8,5,5,4,128]{4,3,2,1,0:T(4,128)S(1)}, f32[8,5,5,4,128]{4,3,2,1,0:T(4,128)}, u32[]{:S(2)}) copy-start(f32[8,5,5,4,128]{4,3,2,1,0:T(4,128)} %param.4) | copy-start | bytes 1228804
  1.0 0.9 %copy-start.1 = (f32[3,8,5,4,128]{4,3,2,1,0:T(4,128)S(1)}, f32[3,8,5,4,128]{4,3,2,1,0:T(4,128)}, u32[]{:S(2)}) copy-start(f32[3,8,5,4,128]{4,3,2,1,0:T(4,128)} %param.3) | copy-start | bytes 737284
  1.9 0.7 %copy-start.2 = (f32[8,4,128]{2,1,0:T(4,128)S(1)}, f32[8,4,128]{2,1,0:T(4,128)}, u32[]{:S(2)}) copy-start(f32[8,4,128]{2,1,0:T(4,128)} %diss_hbm.1) | copy-start | bytes 49156

commit v2 on v1

--- a/solution.py
+++ b/solution.py
@@ -17,7 +17,9 @@
 GL, GR, CC = 0, NSYM, 2 * NSYM
 NMAT = 2 * NSYM + B * B
 MROWS = 56
+SOLVERS = ((2, 3, 4, 5), (12, 13, 14, 15))
 GROWS = 16
+GSEND = 2 * B
 
 
 def total(terms):
@@ -118,16 +120,27 @@
     pz = lax.axis_index("pz")
     core = lax.rem(py, 2)
     ncell = jv.shape[0] // (B * B)
-    solver = [4 * s + 2 * core for s in range(4)]
-    is_solver = lax.rem(p + n - 2 * core, 4) == 0
-    mine = lax.div(p, 4)
+    solver = [jnp.where(core == 0, SOLVERS[0][s], SOLVERS[1][s]) for s in range(4)]
+    mine = sum(jnp.where(p == solver[s], s, 0) for s in range(4))
+    solvers_here = sum(jnp.where(p == solver[s], 1, 0) for s in range(4))
+    is_solver = solvers_here > 0
 
     barrier = pltpu.get_barrier_semaphore()
-    peers = [{"line": lax.rem(p + o, n)} for o in range(1, n)]
+    peers = [{"line": lax.rem(p + o, n)} for o in (1, n - 1)]
     peers += [{"py": lax.rem(py + o, npy)} for o in (1, npy - 1)]
     peers += [{"pz": lax.rem(pz + o, npz)} for o in (1, npz - 1)]
     for peer in peers:
         pl.semaphore_signal(barrier, inc=1, device_id=peer, device_id_type=MESH)
+
+    def greet_line():
+        def one(o, carry):
+            far = {"line": lax.rem(p + o, n)}
+            pl.semaphore_signal(barrier, inc=1, device_id=far, device_id_type=MESH)
+            return carry
+
+        lax.fori_loop(1, n, one, 0)
+
+    pl.when(is_solver)(greet_line)
 
     loads = [
         pltpu.make_async_copy(flux_hbm, fv, lsem.at[0]),
@@ -189,6 +202,29 @@
         return carry
 
     lax.fori_loop(0, ncell // 2, first_level, 0)
+
+    pl.semaphore_wait(barrier, len(peers) + 4 - solvers_here)
+
+    halo = []
+
+    def send_halo(src, dst, index, peer):
+        copy = pltpu.make_async_remote_copy(
+            src_ref=src,
+            dst_ref=dst,
+            send_sem=hsend.at[index],
+            recv_sem=hrecv.at[index],
+            device_id=peer,
+            device_id_type=MESH,
+        )
+        copy.start()
+        halo.append(copy)
+
+    send_halo(fv.at[0, pl.ds(ncomp - B, B)], xl, 0, {"line": lax.rem(p + 1, n)})
+    send_halo(fv.at[0, pl.ds(0, B)], xr, 1, {"line": lax.rem(p + n - 1, n)})
+    send_halo(ysr, yl, 2, {"py": lax.rem(py + 1, npy)})
+    send_halo(ysl, yr, 3, {"py": lax.rem(py + npy - 1, npy)})
+    send_halo(zsr, zl, 4, {"pz": lax.rem(pz + 1, npz)})
+    send_halo(zsl, zr, 5, {"pz": lax.rem(pz + npz - 1, npz)})
 
     def merge(i, carry):
         a, b, new = 2 * i * NMAT, (2 * i + 1) * NMAT, (4 + i) * NMAT
@@ -224,32 +260,9 @@
             value = value + diag0
         msend[pl.ds(e, 4, stride=MROWS), :] = value
 
-    pl.semaphore_wait(barrier, len(peers))
-
-    halo = []
-
-    def send_halo(src, dst, index, peer):
-        copy = pltpu.make_async_remote_copy(
-            src_ref=src,
-            dst_ref=dst,
-            send_sem=hsend.at[index],
-            recv_sem=hrecv.at[index],
-            device_id=peer,
-            device_id_type=MESH,
-        )
-        copy.start()
-        halo.append(copy)
-
-    send_halo(fv.at[0, pl.ds(ncomp - B, B)], xl, 0, {"line": lax.rem(p + 1, n)})
-    send_halo(fv.at[0, pl.ds(0, B)], xr, 1, {"line": lax.rem(p + n - 1, n)})
-    send_halo(ysr, yl, 2, {"py": lax.rem(py + 1, npy)})
-    send_halo(ysl, yr, 3, {"py": lax.rem(py + npy - 1, npy)})
-    send_halo(zsr, zl, 4, {"pz": lax.rem(pz + 1, npz)})
-    send_halo(zsl, zr, 5, {"pz": lax.rem(pz + npz - 1, npz)})
-
-    def part_copies(src, dst, rows, send_sem, recv_sem, s):
-        here = src.at[pl.ds(s * rows, rows)]
-        there = dst.at[pl.ds(pl.multiple_of(p * rows, 8), rows)]
+    def part_copies(src, dst, rows, sent, send_sem, recv_sem, s):
+        here = src.at[pl.ds(s * rows, sent)]
+        there = dst.at[pl.ds(pl.multiple_of(p * rows, 8), sent)]
         away = pltpu.make_async_remote_copy(
             src_ref=here,
             dst_ref=there,
@@ -260,23 +273,23 @@
         )
         return away, pltpu.make_async_copy(here, there, send_sem.at[s])
 
-    def start_parts(src, dst, rows, send_sem, recv_sem):
+    def start_parts(src, dst, rows, sent, send_sem, recv_sem):
         for s in range(4):
-            away, near = part_copies(src, dst, rows, send_sem, recv_sem, s)
+            away, near = part_copies(src, dst, rows, sent, send_sem, recv_sem, s)
             pl.when(solver[s] != p)(away.start)
             pl.when(solver[s] == p)(near.start)
 
-    def finish_parts(src, dst, rows, send_sem, recv_sem):
+    def finish_parts(src, dst, rows, sent, send_sem, recv_sem):
         for s in range(4):
-            away, near = part_copies(src, dst, rows, send_sem, recv_sem, s)
+            away, near = part_copies(src, dst, rows, sent, send_sem, recv_sem, s)
             pl.when(solver[s] != p)(away.wait_send)
             pl.when(solver[s] == p)(near.wait)
 
-    def await_parts(src, dst, rows, send_sem, recv_sem):
+    def await_parts(src, dst, rows, sent, send_sem, recv_sem):
         def one(q, carry):
             copy = pltpu.make_async_remote_copy(
-                src_ref=src.at[pl.ds(0, rows)],
-                dst_ref=dst.at[pl.ds(pl.multiple_of(q * rows, 8), rows)],
+                src_ref=src.at[pl.ds(0, sent)],
+                dst_ref=dst.at[pl.ds(pl.multiple_of(q * rows, 8), sent)],
                 send_sem=send_sem.at[0],
                 recv_sem=recv_sem.at[q],
                 device_id={"line": solver[0]},
@@ -287,8 +300,8 @@
 
         lax.fori_loop(0, n, one, 0)
 
-    mats = (msend, mrecv, MROWS, m_s, m_r)
-    sides = (gsend, grecv, GROWS, g_s, g_r)
+    mats = (msend, mrecv, MROWS, NMAT, m_s, m_r)
+    sides = (gsend, grecv, GROWS, GSEND, g_s, g_r)
     start_parts(*mats)
 
     for copy in halo:
@@ -555,7 +568,7 @@
             dma((4,)),
         ],
         compiler_params=pltpu.CompilerParams(
-            collective_id=0, has_side_effects=True, vmem_limit_bytes=32 * 1024 * 1024
+            collective_id=0, has_side_effects=True, vmem_limit_bytes=60 * 1024 * 1024
         ),
     )(
         fluxes.reshape((3, ncomp) + tail),

time: 39.9 us -> 35.8 us (0.90)
  the two profiles are of different devices: /device:TPU:24 before, /device:TPU:31 now
where the time goes in v2:
time: 35.8 us; the launch traced here: 35.7 us
  Pallas kernels  34.1 us (95%)
  local copies, waits for them, and re-layouts  1.53 us (4%)
    pallas_call x1, Pallas kernels, per_device(): pl.pallas_call(functools.partial(kernel, n, npy, npz), out_shape=jax.Shap...  34.1 us
    unnamed x1, local copies, waits for them, and re-layouts  1.53 us

profile of v2, /device:TPU:31, one launch (start us, length us, event | category | flops | bytes accessed | tf_op | source)
XLA Modules:
  0.0 35.7 jit_solution(1338983833552160192)
XLA Ops:
  0.0 34.1 %shard_map.37 = f32[40,4,128]{2,1,0:T(4,128)} custom-call(f32[3,40,4,128]{3,2,1,0:T(4,128)} %bitcast.5, f32[200,4,128]{2,1,0:T(4,128)} %bitcast.3, f32[8,4,128]{2,1,0:T(4,128)} %diss_hbm.1), custom_call_target="tpu_custom_call" | custom-call | tf_op jit(solution)/shard_map/pallas_call | solution.py:529
  34.1 1.5 %copy.5 = f32[8,5,4,128]{3,2,1,0:T(4,128)} copy(f32[8,5,4,128]{3,2,1,0:T(4,128)} %bitcast.4) | data formatting | bytes 163840

commit v3 on v1

--- a/solution.py
+++ b/solution.py
@@ -17,7 +17,9 @@
 GL, GR, CC = 0, NSYM, 2 * NSYM
 NMAT = 2 * NSYM + B * B
 MROWS = 56
+SOLVERS = ((12, 13, 14, 15), (1, 3, 5, 7))
 GROWS = 16
+GSEND = 2 * B
 
 
 def total(terms):
@@ -118,14 +120,21 @@
     pz = lax.axis_index("pz")
     core = lax.rem(py, 2)
     ncell = jv.shape[0] // (B * B)
-    solver = [4 * s + 2 * core for s in range(4)]
-    is_solver = lax.rem(p + n - 2 * core, 4) == 0
-    mine = lax.div(p, 4)
+    solver = [jnp.where(core == 0, SOLVERS[0][s], SOLVERS[1][s]) for s in range(4)]
+    mine = sum(jnp.where(p == solver[s], s, 0) for s in range(4))
+    solvers_here = sum(jnp.where(p == solver[s], 1, 0) for s in range(4))
+    is_solver = solvers_here > 0
 
     barrier = pltpu.get_barrier_semaphore()
-    peers = [{"line": lax.rem(p + o, n)} for o in range(1, n)]
+    peers = [{"line": lax.rem(p + o, n)} for o in (1, n - 1)]
     peers += [{"py": lax.rem(py + o, npy)} for o in (1, npy - 1)]
     peers += [{"pz": lax.rem(pz + o, npz)} for o in (1, npz - 1)]
+    def greet_line():
+        for t in range(1, n):
+            far = {"line": lax.rem(p + n // 2 + (t // 2 if t % 2 else n - t // 2), n)}
+            pl.semaphore_signal(barrier, inc=1, device_id=far, device_id_type=MESH)
+
+    pl.when(is_solver)(greet_line)
     for peer in peers:
         pl.semaphore_signal(barrier, inc=1, device_id=peer, device_id_type=MESH)
 
@@ -136,7 +145,6 @@
     ]
     for load in loads:
         load.start()
-    sol[...] = jnp.zeros_like(sol)
     msend[...] = jnp.zeros_like(msend)
     gsend[...] = jnp.zeros_like(gsend)
     ncomp = ncell * B
@@ -224,7 +232,7 @@
             value = value + diag0
         msend[pl.ds(e, 4, stride=MROWS), :] = value
 
-    pl.semaphore_wait(barrier, len(peers))
+    pl.semaphore_wait(barrier, len(peers) + 4 - solvers_here)
 
     halo = []
 
@@ -247,9 +255,9 @@
     send_halo(zsr, zl, 4, {"pz": lax.rem(pz + 1, npz)})
     send_halo(zsl, zr, 5, {"pz": lax.rem(pz + npz - 1, npz)})
 
-    def part_copies(src, dst, rows, send_sem, recv_sem, s):
-        here = src.at[pl.ds(s * rows, rows)]
-        there = dst.at[pl.ds(pl.multiple_of(p * rows, 8), rows)]
+    def part_copies(src, dst, rows, sent, send_sem, recv_sem, s):
+        here = src.at[pl.ds(s * rows, sent)]
+        there = dst.at[pl.ds(pl.multiple_of(p * rows, 8), sent)]
         away = pltpu.make_async_remote_copy(
             src_ref=here,
             dst_ref=there,
@@ -260,23 +268,23 @@
         )
         return away, pltpu.make_async_copy(here, there, send_sem.at[s])
 
-    def start_parts(src, dst, rows, send_sem, recv_sem):
+    def start_parts(src, dst, rows, sent, send_sem, recv_sem):
         for s in range(4):
-            away, near = part_copies(src, dst, rows, send_sem, recv_sem, s)
+            away, near = part_copies(src, dst, rows, sent, send_sem, recv_sem, s)
             pl.when(solver[s] != p)(away.start)
             pl.when(solver[s] == p)(near.start)
 
-    def finish_parts(src, dst, rows, send_sem, recv_sem):
+    def finish_parts(src, dst, rows, sent, send_sem, recv_sem):
         for s in range(4):
-            away, near = part_copies(src, dst, rows, send_sem, recv_sem, s)
+            away, near = part_copies(src, dst, rows, sent, send_sem, recv_sem, s)
             pl.when(solver[s] != p)(away.wait_send)
             pl.when(solver[s] == p)(near.wait)
 
-    def await_parts(src, dst, rows, send_sem, recv_sem):
+    def await_parts(src, dst, rows, sent, send_sem, recv_sem):
         def one(q, carry):
             copy = pltpu.make_async_remote_copy(
-                src_ref=src.at[pl.ds(0, rows)],
-                dst_ref=dst.at[pl.ds(pl.multiple_of(q * rows, 8), rows)],
+                src_ref=src.at[pl.ds(0, sent)],
+                dst_ref=dst.at[pl.ds(pl.multiple_of(q * rows, 8), sent)],
                 send_sem=send_sem.at[0],
                 recv_sem=recv_sem.at[q],
                 device_id={"line": solver[0]},
@@ -287,8 +295,8 @@
 
         lax.fori_loop(0, n, one, 0)
 
-    mats = (msend, mrecv, MROWS, m_s, m_r)
-    sides = (gsend, grecv, GROWS, g_s, g_r)
+    mats = (msend, mrecv, MROWS, NMAT, m_s, m_r)
+    sides = (gsend, grecv, GROWS, GSEND, g_s, g_r)
     start_parts(*mats)
 
     for copy in halo:
@@ -346,8 +354,8 @@
 
     def answer_copy(q):
         return pltpu.make_async_remote_copy(
-            src_ref=sol.at[pl.ds(pl.multiple_of(q * 8, 8), 16)],
-            dst_ref=xrecv.at[pl.ds(pl.multiple_of(mine * 16, 16), 16)],
+            src_ref=sol.at[pl.ds(pl.multiple_of(q * GROWS, 16), GSEND)],
+            dst_ref=xrecv.at[pl.ds(pl.multiple_of(mine * GROWS, 16), GSEND)],
             send_sem=x_s.at[q],
             recv_sem=x_r.at[mine],
             device_id={"line": q},
@@ -355,8 +363,8 @@
         )
 
     own_answer = pltpu.make_async_copy(
-        sol.at[pl.ds(pl.multiple_of(p * 8, 8), 16)],
-        xrecv.at[pl.ds(pl.multiple_of(mine * 16, 16), 16)],
+        sol.at[pl.ds(pl.multiple_of(p * GROWS, 16), GSEND)],
+        xrecv.at[pl.ds(pl.multiple_of(mine * GROWS, 16), GSEND)],
         x_s.at[p],
     )
 
@@ -443,8 +451,11 @@
         from_l = mat_vec(w0, x_even)
         from_r = mat_vec(u0, x_next)
         for c in range(B):
-            sol[pl.ds(c, 8, stride=16), :] = x_even[c]
-            sol[pl.ds(8 + c, 8, stride=16), :] = own[c] + from_l[c] + from_r[c]
+            x_odd = own[c] + from_l[c] + from_r[c]
+            sol[pl.ds(c, 8, stride=2 * GROWS), :] = x_even[c]
+            sol[pl.ds(B + c, 8, stride=2 * GROWS), :] = x_odd
+            sol[pl.ds(GROWS + c, 8, stride=2 * GROWS), :] = x_odd
+            sol[pl.ds(GROWS + B + c, 8, stride=2 * GROWS), :] = x_next[c]
 
         def send_one(q, carry):
             pl.when(q != p)(answer_copy(q).start)
@@ -458,8 +469,8 @@
 
     for s in range(4):
         copy = pltpu.make_async_remote_copy(
-            src_ref=sol.at[pl.ds(0, 16)],
-            dst_ref=xrecv.at[pl.ds(s * 16, 16)],
+            src_ref=sol.at[pl.ds(0, GSEND)],
+            dst_ref=xrecv.at[pl.ds(s * GROWS, GSEND)],
             send_sem=x_s.at[0],
             recv_sem=x_r.at[s],
             device_id={"line": solver[s]},
@@ -468,8 +479,8 @@
         pl.when(solver[s] != p)(copy.wait_recv)
 
     x = [None] * (ncell + 1)
-    x[0] = [xrecv[pl.ds(c, 4, stride=16), :] for c in range(B)]
-    x[ncell] = [xrecv[pl.ds(8 + c, 4, stride=16), :] for c in range(B)]
+    x[0] = [xrecv[pl.ds(c, 4, stride=GROWS), :] for c in range(B)]
+    x[ncell] = [xrecv[pl.ds(B + c, 4, stride=GROWS), :] for c in range(B)]
     for i, (m, a, b) in ((2, (4, 0, 8)), (0, (2, 0, 4)), (1, (6, 4, 8))):
         w = as_mat([facs[i * 65 + NSYM + e] for e in range(B * B)])
         u = as_mat([facs[i * 65 + NSYM + B * B + e] for e in range(B * B)])
@@ -542,8 +553,8 @@
             flat(4 * GROWS),
             flat(n * GROWS),
             vmem((256, 8, 128), f32),
-            flat((n + 1) * 8),
-            flat(4 * 16),
+            flat(n * GROWS),
+            flat(4 * GROWS),
             dma((3,)),
             dma((6,)),
             dma((6,)),
@@ -555,7 +566,7 @@
             dma((4,)),
         ],
         compiler_params=pltpu.CompilerParams(
-            collective_id=0, has_side_effects=True, vmem_limit_bytes=32 * 1024 * 1024
+            collective_id=0, has_side_effects=True, vmem_limit_bytes=60 * 1024 * 1024
         ),
     )(
         fluxes.reshape((3, ncomp) + tail),

time: 39.9 us -> 34.6 us (0.87)
  Pallas kernels: 36.2 us -> 32.8 us
  local copies, waits for them, and re-layouts: 3.3 us -> 1.53 us
    pallas_call x1, Pallas kernels: 36.2 us -> 32.8 us  [per_device(): pl.pallas_call(functools.partial(kernel, n, npy, npz), out_shape=jax.Shap...]
    unnamed x7 -> x1, local copies, waits for them, and re-layouts: 3.3 us -> 1.53 us
where the time goes in v3:
time: 34.6 us; the launch traced here: 34.4 us
  Pallas kernels  32.8 us (95%)
  local copies, waits for them, and re-layouts  1.53 us (4%)
    pallas_call x1, Pallas kernels, per_device(): pl.pallas_call(functools.partial(kernel, n, npy, npz), out_shape=jax.Shap...  32.8 us
    unnamed x1, local copies, waits for them, and re-layouts  1.53 us

profile of v3, /device:TPU:24, one launch (start us, length us, event | category | flops | bytes accessed | tf_op | source)
XLA Modules:
  0.0 34.4 jit_solution(1553011764121867839)
XLA Ops:
  0.0 32.8 %shard_map.37 = f32[40,4,128]{2,1,0:T(4,128)} custom-call(f32[3,40,4,128]{3,2,1,0:T(4,128)} %bitcast.5, f32[200,4,128]{2,1,0:T(4,128)} %bitcast.3, f32[8,4,128]{2,1,0:T(4,128)} %diss_hbm.1), custom_call_target="tpu_custom_call" | custom-call | tf_op jit(solution)/shard_map/pallas_call | solution.py:527
  32.8 1.5 %copy.5 = f32[8,5,4,128]{3,2,1,0:T(4,128)} copy(f32[8,5,4,128]{3,2,1,0:T(4,128)} %bitcast.4) | data formatting | bytes 163840

commit v4 on v3

--- a/solution.py
+++ b/solution.py
@@ -17,7 +17,7 @@
 GL, GR, CC = 0, NSYM, 2 * NSYM
 NMAT = 2 * NSYM + B * B
 MROWS = 56
-SOLVERS = ((12, 13, 14, 15), (1, 3, 5, 7))
+SOLVERS = ((12, 13, 14, 15), (1, 2, 3, 4))
 GROWS = 16
 GSEND = 2 * B
 

time: 34.6 us -> 34 us (0.983)
  Pallas kernels: 32.8 us -> 32.3 us
    pallas_call x1, Pallas kernels: 32.8 us -> 32.3 us  [per_device(): pl.pallas_call(functools.partial(kernel, n, npy, npz), out_shape=jax.Shap...]
where the time goes in v4:
time: 34 us; the launch traced here: 33.8 us
  Pallas kernels  32.3 us (95%)
  local copies, waits for them, and re-layouts  1.53 us (4%)
    pallas_call x1, Pallas kernels, per_device(): pl.pallas_call(functools.partial(kernel, n, npy, npz), out_shape=jax.Shap...  32.3 us
    unnamed x1, local copies, waits for them, and re-layouts  1.53 us

profile of v4, /device:TPU:24, one launch (start us, length us, event | category | flops | bytes accessed | tf_op | source)
XLA Modules:
  0.0 33.8 jit_solution(8385408246791076424)
XLA Ops:
  0.0 32.3 %shard_map.37 = f32[40,4,128]{2,1,0:T(4,128)} custom-call(f32[3,40,4,128]{3,2,1,0:T(4,128)} %bitcast.5, f32[200,4,128]{2,1,0:T(4,128)} %bitcast.3, f32[8,4,128]{2,1,0:T(4,128)} %diss_hbm.1), custom_call_target="tpu_custom_call" | custom-call | tf_op jit(solution)/shard_map/pallas_call | solution.py:527
  32.3 1.5 %copy.5 = f32[8,5,4,128]{3,2,1,0:T(4,128)} copy(f32[8,5,4,128]{3,2,1,0:T(4,128)} %bitcast.4) | data formatting | bytes 163840

commit v5 on v4

--- a/solution.py
+++ b/solution.py
@@ -566,7 +566,7 @@
             dma((4,)),
         ],
         compiler_params=pltpu.CompilerParams(
-            collective_id=0, has_side_effects=True, vmem_limit_bytes=60 * 1024 * 1024
+            collective_id=0, has_side_effects=True, vmem_limit_bytes=54936 * 1024
         ),
     )(
         fluxes.reshape((3, ncomp) + tail),

time: 34 us -> 33.2 us (0.976)
  Pallas kernels: 32.3 us -> 31.7 us
    pallas_call x1, Pallas kernels: 32.3 us -> 31.7 us  [per_device(): pl.pallas_call(functools.partial(kernel, n, npy, npz), out_shape=jax.Shap...]
    unnamed x1 -> x3, local copies, waits for them, and re-layouts: 1.53 us -> 1.35 us
where the time goes in v5:
time: 33.2 us; the launch traced here: 33 us
  Pallas kernels  31.7 us (95%)
  local copies, waits for them, and re-layouts  1.35 us (4%)
    pallas_call x1, Pallas kernels, per_device(): pl.pallas_call(functools.partial(kernel, n, npy, npz), out_shape=jax.Shap...  31.7 us
    unnamed x3, local copies, waits for them, and re-layouts  1.35 us

profile of v5, /device:TPU:24, one launch (start us, length us, event | category | flops | bytes accessed | tf_op | source)
XLA Modules:
  0.0 33.0 jit_solution(12957229590053005978)
XLA Ops:
  0.0 0.0 copy-start
  0.0 0.7 %copy-done = f32[8,4,128]{2,1,0:T(4,128)S(1)} copy-done((f32[8,4,128]{2,1,0:T(4,128)S(1)}, f32[8,4,128]{2,1,0:T(4,128)}, u32[]{:S(2)}) %copy-start) | copy-done | bytes 16408
  0.7 31.7 %shard_map.37 = f32[40,4,128]{2,1,0:T(4,128)S(1)} custom-call(f32[3,40,4,128]{3,2,1,0:T(4,128)} %bitcast.5, f32[200,4,128]{2,1,0:T(4,128)} %bitcast.4, f32[8,4,128]{2,1,0:T(4,128)S(1)} %copy-done), custom_call_target="tpu_custom_call" | custom-call | tf_op jit(solution)/shard_map/pallas_call | solution.py:527
  32.4 0.6 %copy.5 = f32[8,5,4,128]{3,2,1,0:T(4,128)} copy(f32[8,5,4,128]{3,2,1,0:T(4,128)S(1)} %bitcast.3) | data formatting | bytes 163840
Async XLA Ops:
  0.0 0.7 %copy-start = (f32[8,4,128]{2,1,0:T(4,128)S(1)}, f32[8,4,128]{2,1,0:T(4,128)}, u32[]{:S(2)}) copy-start(f32[8,4,128]{2,1,0:T(4,128)} %diss_hbm.1) | copy-start | bytes 49156

commit v6 on v5

--- a/solution.py
+++ b/solution.py
@@ -17,7 +17,7 @@
 GL, GR, CC = 0, NSYM, 2 * NSYM
 NMAT = 2 * NSYM + B * B
 MROWS = 56
-SOLVERS = ((12, 13, 14, 15), (1, 2, 3, 4))
+SOLVERS = ((12, 13, 14, 15), (1, 2, 4, 6))
 GROWS = 16
 GSEND = 2 * B
 
@@ -129,15 +129,6 @@
     peers = [{"line": lax.rem(p + o, n)} for o in (1, n - 1)]
     peers += [{"py": lax.rem(py + o, npy)} for o in (1, npy - 1)]
     peers += [{"pz": lax.rem(pz + o, npz)} for o in (1, npz - 1)]
-    def greet_line():
-        for t in range(1, n):
-            far = {"line": lax.rem(p + n // 2 + (t // 2 if t % 2 else n - t // 2), n)}
-            pl.semaphore_signal(barrier, inc=1, device_id=far, device_id_type=MESH)
-
-    pl.when(is_solver)(greet_line)
-    for peer in peers:
-        pl.semaphore_signal(barrier, inc=1, device_id=peer, device_id_type=MESH)
-
     loads = [
         pltpu.make_async_copy(flux_hbm, fv, lsem.at[0]),
         pltpu.make_async_copy(jac_hbm, jv, lsem.at[1]),
@@ -145,6 +136,16 @@
     ]
     for load in loads:
         load.start()
+
+    def greet_line():
+        for t in range(1, n):
+            far = {"line": lax.rem(p + n // 2 + (t // 2 if t % 2 else n - t // 2), n)}
+            pl.semaphore_signal(barrier, inc=1, device_id=far, device_id_type=MESH)
+
+    pl.when(is_solver)(greet_line)
+    for peer in peers:
+        pl.semaphore_signal(barrier, inc=1, device_id=peer, device_id_type=MESH)
+
     msend[...] = jnp.zeros_like(msend)
     gsend[...] = jnp.zeros_like(gsend)
     ncomp = ncell * B

time: 33.2 us -> 33.2 us (level)
  no operation moved by 1% of the time
where the time goes in v6:
time: 33.2 us; the launch traced here: 33 us
  Pallas kernels  31.6 us (95%)
  local copies, waits for them, and re-layouts  1.35 us (4%)
    pallas_call x1, Pallas kernels, per_device(): pl.pallas_call(functools.partial(kernel, n, npy, npz), out_shape=jax.Shap...  31.6 us
    unnamed x3, local copies, waits for them, and re-layouts  1.35 us

profile of v6, /device:TPU:24, one launch (start us, length us, event | category | flops | bytes accessed | tf_op | source)
XLA Modules:
  0.0 33.0 jit_solution(9546837802390003218)
XLA Ops:
  0.0 0.0 copy-start
  0.0 0.7 %copy-done = f32[8,4,128]{2,1,0:T(4,128)S(1)} copy-done((f32[8,4,128]{2,1,0:T(4,128)S(1)}, f32[8,4,128]{2,1,0:T(4,128)}, u32[]{:S(2)}) %copy-start) | copy-done | bytes 16408
  0.7 31.6 %shard_map.37 = f32[40,4,128]{2,1,0:T(4,128)S(1)} custom-call(f32[3,40,4,128]{3,2,1,0:T(4,128)} %bitcast.5, f32[200,4,128]{2,1,0:T(4,128)} %bitcast.4, f32[8,4,128]{2,1,0:T(4,128)S(1)} %copy-done), custom_call_target="tpu_custom_call" | custom-call | tf_op jit(solution)/shard_map/pallas_call | solution.py:528
  32.4 0.6 %copy.5 = f32[8,5,4,128]{3,2,1,0:T(4,128)} copy(f32[8,5,4,128]{3,2,1,0:T(4,128)S(1)} %bitcast.3) | data formatting | bytes 163840
Async XLA Ops:
  0.0 0.7 %copy-start = (f32[8,4,128]{2,1,0:T(4,128)S(1)}, f32[8,4,128]{2,1,0:T(4,128)}, u32[]{:S(2)}) copy-start(f32[8,4,128]{2,1,0:T(4,128)} %diss_hbm.1) | copy-start | bytes 49156

commit v7 on v6

--- a/solution.py
+++ b/solution.py
@@ -275,11 +275,15 @@
             pl.when(solver[s] != p)(away.start)
             pl.when(solver[s] == p)(near.start)
 
-    def finish_parts(src, dst, rows, sent, send_sem, recv_sem):
+    def finish_home(src, dst, rows, sent, send_sem, recv_sem):
         for s in range(4):
-            away, near = part_copies(src, dst, rows, sent, send_sem, recv_sem, s)
+            _, near = part_copies(src, dst, rows, sent, send_sem, recv_sem, s)
+            pl.when(solver[s] == p)(near.wait)
+
+    def finish_away(src, dst, rows, sent, send_sem, recv_sem):
+        for s in range(4):
+            away, _ = part_copies(src, dst, rows, sent, send_sem, recv_sem, s)
             pl.when(solver[s] != p)(away.wait_send)
-            pl.when(solver[s] == p)(near.wait)
 
     def await_parts(src, dst, rows, sent, send_sem, recv_sem):
         def one(q, carry):
@@ -370,7 +374,7 @@
     )
 
     def solve():
-        finish_parts(*mats)
+        finish_home(*mats)
         await_parts(*mats)
 
         def even(e):
@@ -419,7 +423,7 @@
                 couple = [[pltpu.roll(v, 8 - step, 0) for v in line] for line in product(couple, w)]
         at_last = keep(sym_inverse(diag))
 
-        finish_parts(*sides)
+        finish_home(*sides)
         await_parts(*sides)
 
         def saved(start, count):
@@ -500,11 +504,8 @@
     for copy in halo:
         copy.wait_send()
 
-    def others():
-        finish_parts(*mats)
-        finish_parts(*sides)
-
-    pl.when(jnp.logical_not(is_solver))(others)
+    finish_away(*mats)
+    finish_away(*sides)
 
     def answers_sent():
         def one(q, carry):

time: 33.2 us -> 33.2 us (level)
  no operation moved by 1% of the time
where the time goes in v7:
time: 33.2 us; the launch traced here: 33 us
  Pallas kernels  31.6 us (95%)
  local copies, waits for them, and re-layouts  1.35 us (4%)
    pallas_call x1, Pallas kernels, per_device(): pl.pallas_call(functools.partial(kernel, n, npy, npz), out_shape=jax.Shap...  31.6 us
    unnamed x3, local copies, waits for them, and re-layouts  1.35 us

profile of v7, /device:TPU:24, one launch (start us, length us, event | category | flops | bytes accessed | tf_op | source)
XLA Modules:
  0.0 33.0 jit_solution(3311432732087367645)
XLA Ops:
  0.0 0.0 copy-start
  0.0 0.7 %copy-done = f32[8,4,128]{2,1,0:T(4,128)S(1)} copy-done((f32[8,4,128]{2,1,0:T(4,128)S(1)}, f32[8,4,128]{2,1,0:T(4,128)}, u32[]{:S(2)}) %copy-start) | copy-done | bytes 16408
  0.7 31.6 %shard_map.37 = f32[40,4,128]{2,1,0:T(4,128)S(1)} custom-call(f32[3,40,4,128]{3,2,1,0:T(4,128)} %bitcast.5, f32[200,4,128]{2,1,0:T(4,128)} %bitcast.4, f32[8,4,128]{2,1,0:T(4,128)S(1)} %copy-done), custom_call_target="tpu_custom_call" | custom-call | tf_op jit(solution)/shard_map/pallas_call | solution.py:529
  32.4 0.6 %copy.5 = f32[8,5,4,128]{3,2,1,0:T(4,128)} copy(f32[8,5,4,128]{3,2,1,0:T(4,128)S(1)} %bitcast.3) | data formatting | bytes 163840
Async XLA Ops:
  0.0 0.7 %copy-start = (f32[8,4,128]{2,1,0:T(4,128)S(1)}, f32[8,4,128]{2,1,0:T(4,128)}, u32[]{:S(2)}) copy-start(f32[8,4,128]{2,1,0:T(4,128)} %diss_hbm.1) | copy-start | bytes 49156
